TPU v7x, 1024 devices: a whole 4x8x16 slice. The times are simulated.
1024 devices in a mesh: sx: 16 (over y_hi, x, core), sy: 4 (over y_lo), cr: 16 (over z).
Axes of the slice: x: 4, y: 8 (y_hi: 2, y_lo: 4; y = y_hi * 4 + y_lo), z: 16, core: 2. Of those that a mesh axis runs over, the one named last changes fastest.
Arguments:
- adjoint: float32 [256, 256, 512], P('cr', 'sx', 'sy'), may hold values from -6 to 6
- sensor_rows: bfloat16 [12288, 256, 512], P('cr', 'sx', 'sy'), may hold values from -0.015625 to 0.015625
- cell_ids: int32 [256, 512], P('sx', 'sy'), may hold values from 0 to 15
- mat_diag: float32 [16], replicated, may hold values from -0.15 to 0.15
- mat_cond: float32 [16], replicated, may hold values from 0.2 to 0.45
- cheb_coef: float32 [9], replicated, may hold values from 0.3 to 1
Outputs:
- smoothed: float32 [256, 256, 512], P('cr', 'sx', 'sy')
- panel: float32 [12288, 256], P('cr', ('sx', 'sy'))
All inputs are finite; a program needn't handle non-finite values.
Results may differ from a plain program's by a relative error of at most 0.0029.
Values may be sent and summed in bfloat16 or wider, within the bound.
A program may use at most 32 MiB of HBM per device.

v0:
```python
import jax
import jax.numpy as jnp
from jax import lax
from jax.sharding import PartitionSpec as P

DEG = 8


def padded(value, sides, width):
    for axis, dim in sides:
        size, length = (lax.axis_size(axis), value.shape[dim])
        up = [(i, (i + 1) % size) for i in range(size - 1)]
        down = [(j, i) for i, j in up]
        last = lax.slice_in_dim(value, length - width, length, axis=dim)
        first = lax.slice_in_dim(value, 0, width, axis=dim)
        before = lax.ppermute(last, axis, up)
        after = lax.ppermute(first, axis, down)
        value = jnp.concatenate([before, value, after], axis=dim)
    return value


def apply_inner(field, diag, cond):
    weighted = cond * field
    beside = weighted[:, :-2, 1:-1] + weighted[:, 2:, 1:-1]
    beside = beside + weighted[:, 1:-1, :-2] + weighted[:, 1:-1, 2:]
    return diag[1:-1, 1:-1] * field[:, 1:-1, 1:-1] + cond[1:-1, 1:-1] * beside


def trim(array, have, want):
    offset = have - want
    return array[..., offset : array.shape[-2] - offset, offset : array.shape[-1] - offset]


def on_device(adjoint, sensor_rows, cell_ids, mat_diag, mat_cond, cheb_coef):
    width_x = adjoint.shape[1]
    width_y = adjoint.shape[2]
    depth = 1
    ids_wide = padded(cell_ids, (("sx", 0), ("sy", 1)), depth)
    materials = jnp.arange(mat_diag.shape[0], dtype=jnp.int32)
    onehot = (ids_wide[None, :, :] == materials[:, None, None]).astype(jnp.float32)
    diag_wide = jnp.sum(onehot * mat_diag[:, None, None], axis=0)
    cond_wide = jnp.sum(onehot * mat_cond[:, None, None], axis=0)
    start_x = lax.axis_index("sx") * width_x - depth
    start_y = lax.axis_index("sy") * width_y - depth
    pos_x = lax.broadcasted_iota(jnp.int32, (width_x + 2 * depth, width_y + 2 * depth), 0) + start_x
    pos_y = lax.broadcasted_iota(jnp.int32, (width_x + 2 * depth, width_y + 2 * depth), 1) + start_y
    inside = (
        (pos_x >= 0)
        & (pos_x < width_x * lax.axis_size("sx"))
        & (pos_y >= 0)
        & (pos_y < width_y * lax.axis_size("sy"))
    )
    inside = inside.astype(jnp.float32)
    previous = adjoint
    current = adjoint
    smoothed = cheb_coef[0] * adjoint
    for block in range(DEG // depth):
        stacked = jnp.stack([previous, current])
        widened = padded(stacked, (("sx", 2), ("sy", 3)), depth)
        prev_wide = widened[0]
        curr_wide = widened[1]
        diag_here = trim(diag_wide, depth, depth)
        cond_here = trim(cond_wide, depth, depth)
        applied = apply_inner(curr_wide, diag_here, cond_here)
        order = block * depth
        if order == 0:
            newer = applied
        else:
            newer = 2.0 * applied - prev_wide[:, 1:-1, 1:-1]
        newer = newer * trim(inside, depth, depth - 1)
        prev_wide = curr_wide[:, 1:-1, 1:-1]
        curr_wide = newer
        smoothed = smoothed + cheb_coef[order + 1] * trim(newer, depth - 1, 0)
        previous = prev_wide
        current = curr_wide
    lowered = smoothed.astype(jnp.bfloat16)
    flat_rows = sensor_rows.reshape(sensor_rows.shape[0], -1)
    piece = lax.all_gather(lowered, "cr", axis=0, tiled=True)
    flat_piece = piece.reshape(piece.shape[0], -1)
    partial_panel = lax.dot_general(
        flat_rows, flat_piece, (((1,), (1,)), ((), ())), preferred_element_type=jnp.float32
    )
    panel = lax.psum_scatter(partial_panel, ("sx", "sy"), scatter_dimension=1, tiled=True)
    return (smoothed, panel)


def solution(mesh):
    placed = (P("cr", "sx", "sy"), P("cr", "sx", "sy"), P("sx", "sy"), P(), P(), P())
    return jax.shard_map(
        on_device,
        mesh=mesh,
        in_specs=placed,
        out_specs=(P("cr", "sx", "sy"), P("cr", ("sx", "sy"))),
        check_vma=False,
    )
```

profile of v0, /device:TPU:56, one launch (start us, length us, event | category | flops | bytes accessed | tf_op | source)
XLA Modules:
  0.0 535.9 jit_solution(2497216817564354600)
XLA Ops:
  8.1 2.0 collective-permute-start
  10.1 9.7 %collective-permute-start.1 = (s32[1,128]{1,0:T(1,128)S(1)}, s32[1,128]{1,0:T(1,128)S(1)}, u32[]{:S(2)}, u32[]{:S(2)}) collective-permute-start(s32[1,128]{1,0:T(1,128)S(1)} %get-tuple-element.77), channel_id=1, source_target_pairs={{64,0},{128,64},{192,128},{256,192},{320,256},{384,320},{448,384},... | collective-permute-start | bytes 1544 | tf_op jit(solution)/shard_map/ppermute | solution.py:17
  20.8 1.9 collective-permute-start.4
  22.7 9.7 %collective-permute-start.5 = (f32[2,16,1,128]{3,1,2,0:T(8,128)S(1)}, f32[2,16,1,128]{3,1,2,0:T(8,128)S(1)}, u32[]{:S(2)}, u32[]{:S(2)}) collective-permute-start(f32[2,16,1,128]{3,1,2,0:T(8,128)S(1)} %get-tuple-element.73), channel_id=1, source_target_pairs={{64,0},{128,64},{192,128},{256,192},{320,256},{384,320},{448,384},... | collective-permute-start | bytes 49160 | tf_op jit(solution)/shard_map/ppermute | solution.py:17
  34.8 4.5 collective-permute-start.3
  43.0 5.0 collective-permute-start.7
  49.0 1.7 collective-permute-done.6
  50.7 1.5 collective-permute-done.7
  52.6 1.9 collective-permute-start.8
  54.5 9.7 %collective-permute-start.9 = (f32[2,16,1,128]{3,1,2,0:T(8,128)S(1)}, f32[2,16,1,128]{3,1,2,0:T(8,128)S(1)}, u32[]{:S(2)}, u32[]{:S(2)}) collective-permute-start(f32[2,16,1,128]{3,1,2,0:T(8,128)S(1)} %get-tuple-element.71), channel_id=1, source_target_pairs={{64,0},{128,64},{192,128},{256,192},{320,256},{384,320},{448,384},... | collective-permute-start | bytes 49160 | tf_op jit(solution)/shard_map/ppermute | solution.py:17
  64.2 1.4 collective-permute-done.9
  67.1 5.0 collective-permute-start.11
  72.1 2.7 collective-permute-done.10
  74.9 1.5 collective-permute-done.11
  77.0 1.9 collective-permute-start.12
  78.9 9.7 %collective-permute-start.13 = (f32[2,16,1,128]{3,1,2,0:T(8,128)S(1)}, f32[2,16,1,128]{3,1,2,0:T(8,128)S(1)}, u32[]{:S(2)}, u32[]{:S(2)}) collective-permute-start(f32[2,16,1,128]{3,1,2,0:T(8,128)S(1)} %get-tuple-element.69), channel_id=1, source_target_pairs={{64,0},{128,64},{192,128},{256,192},{320,256},{384,320},{448,384},... | collective-permute-start | bytes 49160 | tf_op jit(solution)/shard_map/ppermute | solution.py:17
  91.5 5.0 collective-permute-start.15
  96.5 2.7 collective-permute-done.14
  99.3 1.5 collective-permute-done.15
  101.4 1.9 collective-permute-start.16
  103.3 9.7 %collective-permute-start.17 = (f32[2,16,1,128]{3,1,2,0:T(8,128)S(1)}, f32[2,16,1,128]{3,1,2,0:T(8,128)S(1)}, u32[]{:S(2)}, u32[]{:S(2)}) collective-permute-start(f32[2,16,1,128]{3,1,2,0:T(8,128)S(1)} %get-tuple-element.67), channel_id=1, source_target_pairs={{64,0},{128,64},{192,128},{256,192},{320,256},{384,320},{448,384},... | collective-permute-start | bytes 49160 | tf_op jit(solution)/shard_map/ppermute | solution.py:17
  115.9 5.0 collective-permute-start.19
  120.9 2.7 collective-permute-done.18
  123.6 1.5 collective-permute-done.19
  125.8 1.9 collective-permute-start.20
  127.7 9.7 %collective-permute-start.21 = (f32[2,16,1,128]{3,1,2,0:T(8,128)S(1)}, f32[2,16,1,128]{3,1,2,0:T(8,128)S(1)}, u32[]{:S(2)}, u32[]{:S(2)}) collective-permute-start(f32[2,16,1,128]{3,1,2,0:T(8,128)S(1)} %get-tuple-element.65), channel_id=1, source_target_pairs={{64,0},{128,64},{192,128},{256,192},{320,256},{384,320},{448,384},... | collective-permute-start | bytes 49160 | tf_op jit(solution)/shard_map/ppermute | solution.py:17
  140.2 5.0 collective-permute-start.23
  145.3 2.7 collective-permute-done.22
  148.0 1.5 collective-permute-done.23
  150.1 1.9 collective-permute-start.24
  152.1 9.7 %collective-permute-start.25 = (f32[2,16,1,128]{3,1,2,0:T(8,128)S(1)}, f32[2,16,1,128]{3,1,2,0:T(8,128)S(1)}, u32[]{:S(2)}, u32[]{:S(2)}) collective-permute-start(f32[2,16,1,128]{3,1,2,0:T(8,128)S(1)} %get-tuple-element.63), channel_id=1, source_target_pairs={{64,0},{128,64},{192,128},{256,192},{320,256},{384,320},{448,384},... | collective-permute-start | bytes 49160 | tf_op jit(solution)/shard_map/ppermute | solution.py:17
  164.6 5.0 collective-permute-start.27
  169.7 2.7 collective-permute-done.26
  172.4 1.5 collective-permute-done.27
  174.5 1.9 collective-permute-start.28
  176.5 9.7 %collective-permute-start.29 = (f32[2,16,1,128]{3,1,2,0:T(8,128)S(1)}, f32[2,16,1,128]{3,1,2,0:T(8,128)S(1)}, u32[]{:S(2)}, u32[]{:S(2)}) collective-permute-start(f32[2,16,1,128]{3,1,2,0:T(8,128)S(1)} %get-tuple-element.61), channel_id=1, source_target_pairs={{64,0},{128,64},{192,128},{256,192},{320,256},{384,320},{448,384},... | collective-permute-start | bytes 49160 | tf_op jit(solution)/shard_map/ppermute | solution.py:17
  189.0 5.0 collective-permute-start.31
  194.1 2.7 collective-permute-done.30
  196.8 1.5 collective-permute-done.31
  198.9 1.9 collective-permute-start.32
  200.9 9.7 %collective-permute-start.33 = (f32[2,16,1,128]{3,1,2,0:T(8,128)S(1)}, f32[2,16,1,128]{3,1,2,0:T(8,128)S(1)}, u32[]{:S(2)}, u32[]{:S(2)}) collective-permute-start(f32[2,16,1,128]{3,1,2,0:T(8,128)S(1)} %get-tuple-element.59), channel_id=1, source_target_pairs={{64,0},{128,64},{192,128},{256,192},{320,256},{384,320},{448,384},... | collective-permute-start | bytes 49160 | tf_op jit(solution)/shard_map/ppermute | solution.py:17
  213.4 5.0 collective-permute-start.35
  219.2 2.0 collective-permute-done.34
  221.2 1.5 collective-permute-done.35
  223.1 6.5 %fusion.41 = (bf16[16,16,128]{2,0,1:T(8,128)(2,1)}, f32[16,16,128]{2,0,1:T(8,128)S(1)}) fusion(f32[16,128]{1,0:T(8,128)S(1)} %and_convert_fusion, f32[16,18,130]{2,0,1:T(8,128)S(1)} %get-tuple-element.15, f32[16,18,130]{2,0,1:T(8,128)S(1)} %broadcast_multiply_fusion, f32[16,128]{1,0:T(8,128)S(1)} %slice.478, f32[16,18,130]{2,0,1:T(8,128)S(1)} %get-tuple-element.14, ...), kind=kLoop, calls=%fused_computation.146 | loop fusion | flops 884736 | bytes 2056228 | tf_op jit(solution)/shard_map/convert_element_type | solution.py:76
  229.7 85.1 %all-gather.2.cloned.1.call-done = bf16[256,16,128]{2,0,1:T(8,128)(2,1)} async-done(((bf16[16,16,128]{2,0,1:T(8,128)(2,1)}), bf16[256,16,128]{2,0,1:T(8,128)(2,1)}) %all-gather.2.cloned.1.call-update) | async-done | bytes 1048592 | tf_op jit(solution)/shard_map/all_gather | solution.py:78
  314.8 3.1 fusion.2
  320.5 207.2 %all-reduce.3.cloned.1.call-done = f32[768,256]{0,1:T(8,128)} async-done(((f32[768,256]{0,1:T(8,128)}), f32[768,256]{0,1:T(8,128)}) %all-reduce.3.cloned.1.call-update) | async-done | bytes 786448
  (109 shorter events, 36.1 us)
Async XLA Ops:
  7.2 307.6 %copy-start = (bf16[768,16,128]{2,1,0:T(8,128)(2,1)S(1)}, bf16[768,16,128]{2,1,0:T(8,128)(2,1)}, u32[]{:S(2)}) copy-start(bf16[768,16,128]{2,1,0:T(8,128)(2,1)} %param.7) | copy-start | bytes 9437188
  7.2 307.6 %all-gather.2.cloned.1.call-start = ((), (), s32[]{:S(2)}) async-start(), calls=%async_computation | async-start | bytes 1114112 | tf_op jit(solution)/shard_map/all_gather | solution.py:78
  8.1 24.6 %collective-permute-start = (s32[1,128]{1,0:T(1,128)S(1)}, s32[1,128]{1,0:T(1,128)S(1)}, u32[]{:S(2)}, u32[]{:S(2)}) collective-permute-start(s32[1,128]{1,0:T(1,128)S(1)} %get-tuple-element.76), channel_id=1, source_target_pairs={{0,64},{64,128},{128,192},{192,256},{256,320},{320,384},{384,448},... | collective-permute-start | bytes 1544 | tf_op jit(solution)/shard_map/ppermute | solution.py:16
  10.1 22.6 %collective-permute-start.1 = (s32[1,128]{1,0:T(1,128)S(1)}, s32[1,128]{1,0:T(1,128)S(1)}, u32[]{:S(2)}, u32[]{:S(2)}) collective-permute-start(s32[1,128]{1,0:T(1,128)S(1)} %get-tuple-element.77), channel_id=1, source_target_pairs={{64,0},{128,64},{192,128},{256,192},{320,256},{384,320},{448,384},... | collective-permute-start | bytes 1544 | tf_op jit(solution)/shard_map/ppermute | solution.py:17
  20.8 20.7 %collective-permute-start.4 = (f32[2,16,1,128]{3,1,2,0:T(8,128)S(1)}, f32[2,16,1,128]{3,1,2,0:T(8,128)S(1)}, u32[]{:S(2)}, u32[]{:S(2)}) collective-permute-start(f32[2,16,1,128]{3,1,2,0:T(8,128)S(1)} %get-tuple-element.72), channel_id=1, source_target_pairs={{0,64},{64,128},{128,192},{192,256},{256,320},{320,384},{384,448},... | collective-permute-start | bytes 49160 | tf_op jit(solution)/shard_map/ppermute | solution.py:16
  22.7 18.8 %collective-permute-start.5 = (f32[2,16,1,128]{3,1,2,0:T(8,128)S(1)}, f32[2,16,1,128]{3,1,2,0:T(8,128)S(1)}, u32[]{:S(2)}, u32[]{:S(2)}) collective-permute-start(f32[2,16,1,128]{3,1,2,0:T(8,128)S(1)} %get-tuple-element.73), channel_id=1, source_target_pairs={{64,0},{128,64},{192,128},{256,192},{320,256},{384,320},{448,384},... | collective-permute-start | bytes 49160 | tf_op jit(solution)/shard_map/ppermute | solution.py:17
  33.5 5.8 %collective-permute-start.2 = (s32[18,1]{1,0:T(8,128)S(1)}, s32[18,1]{1,0:T(8,128)S(1)}, u32[]{:S(2)}, u32[]{:S(2)}) collective-permute-start(s32[18,1]{1,0:T(8,128)S(1)} %get-tuple-element.74), channel_id=1, source_target_pairs={{0,16},{16,32},{32,48},{1,17},{17,33},{33,49},{2,18},{18,34},{34,5... | collective-permute-start | bytes 224 | tf_op jit(solution)/shard_map/ppermute | solution.py:16
  34.8 5.9 %collective-permute-start.3 = (s32[18,1]{1,0:T(8,128)S(1)}, s32[18,1]{1,0:T(8,128)S(1)}, u32[]{:S(2)}, u32[]{:S(2)}) collective-permute-start(s32[18,1]{1,0:T(8,128)S(1)} %get-tuple-element.75), channel_id=1, source_target_pairs={{16,0},{32,16},{48,32},{17,1},{33,17},{49,33},{18,2},{34,18},{50,3... | collective-permute-start | bytes 224 | tf_op jit(solution)/shard_map/ppermute | solution.py:17
  41.7 9.0 %collective-permute-start.6 = (f32[2,16,18,1]{3,1,2,0:T(8,128)S(1)}, f32[2,16,18,1]{3,1,2,0:T(8,128)S(1)}, u32[]{:S(2)}, u32[]{:S(2)}) collective-permute-start(f32[2,16,18,1]{3,1,2,0:T(8,128)S(1)} %get-tuple-element.56), channel_id=1, source_target_pairs={{0,16},{16,32},{32,48},{1,17},{17,33},{33,49},{2,18},{18,34},{34,5... | collective-permute-start | bytes 6920 | tf_op jit(solution)/shard_map/ppermute | solution.py:16
  43.0 9.2 %collective-permute-start.7 = (f32[2,16,18,1]{3,1,2,0:T(8,128)S(1)}, f32[2,16,18,1]{3,1,2,0:T(8,128)S(1)}, u32[]{:S(2)}, u32[]{:S(2)}) collective-permute-start(f32[2,16,18,1]{3,1,2,0:T(8,128)S(1)} %get-tuple-element.57), channel_id=1, source_target_pairs={{16,0},{32,16},{48,32},{17,1},{33,17},{49,33},{18,2},{34,18},{50,3... | collective-permute-start | bytes 6920 | tf_op jit(solution)/shard_map/ppermute | solution.py:17
  52.6 11.6 %collective-permute-start.8 = (f32[2,16,1,128]{3,1,2,0:T(8,128)S(1)}, f32[2,16,1,128]{3,1,2,0:T(8,128)S(1)}, u32[]{:S(2)}, u32[]{:S(2)}) collective-permute-start(f32[2,16,1,128]{3,1,2,0:T(8,128)S(1)} %get-tuple-element.70), channel_id=1, source_target_pairs={{0,64},{64,128},{128,192},{192,256},{256,320},{320,384},{384,448},... | collective-permute-start | bytes 49160 | tf_op jit(solution)/shard_map/ppermute | solution.py:16
  54.5 11.1 %collective-permute-start.9 = (f32[2,16,1,128]{3,1,2,0:T(8,128)S(1)}, f32[2,16,1,128]{3,1,2,0:T(8,128)S(1)}, u32[]{:S(2)}, u32[]{:S(2)}) collective-permute-start(f32[2,16,1,128]{3,1,2,0:T(8,128)S(1)} %get-tuple-element.71), channel_id=1, source_target_pairs={{64,0},{128,64},{192,128},{256,192},{320,256},{384,320},{448,384},... | collective-permute-start | bytes 49160 | tf_op jit(solution)/shard_map/ppermute | solution.py:17
  65.8 9.1 %collective-permute-start.10 = (f32[2,16,18,1]{3,1,2,0:T(8,128)S(1)}, f32[2,16,18,1]{3,1,2,0:T(8,128)S(1)}, u32[]{:S(2)}, u32[]{:S(2)}) collective-permute-start(f32[2,16,18,1]{3,1,2,0:T(8,128)S(1)} %get-tuple-element.52), channel_id=1, source_target_pairs={{0,16},{16,32},{32,48},{1,17},{17,33},{33,49},{2,18},{18,34},{34,5... | collective-permute-start | bytes 6920 | tf_op jit(solution)/shard_map/ppermute | solution.py:16
  67.1 9.2 %collective-permute-start.11 = (f32[2,16,18,1]{3,1,2,0:T(8,128)S(1)}, f32[2,16,18,1]{3,1,2,0:T(8,128)S(1)}, u32[]{:S(2)}, u32[]{:S(2)}) collective-permute-start(f32[2,16,18,1]{3,1,2,0:T(8,128)S(1)} %get-tuple-element.53), channel_id=1, source_target_pairs={{16,0},{32,16},{48,32},{17,1},{33,17},{49,33},{18,2},{34,18},{50,3... | collective-permute-start | bytes 6920 | tf_op jit(solution)/shard_map/ppermute | solution.py:17
  77.0 11.6 %collective-permute-start.12 = (f32[2,16,1,128]{3,1,2,0:T(8,128)S(1)}, f32[2,16,1,128]{3,1,2,0:T(8,128)S(1)}, u32[]{:S(2)}, u32[]{:S(2)}) collective-permute-start(f32[2,16,1,128]{3,1,2,0:T(8,128)S(1)} %get-tuple-element.68), channel_id=1, source_target_pairs={{0,64},{64,128},{128,192},{192,256},{256,320},{320,384},{384,448},... | collective-permute-start | bytes 49160 | tf_op jit(solution)/shard_map/ppermute | solution.py:16
  78.9 11.1 %collective-permute-start.13 = (f32[2,16,1,128]{3,1,2,0:T(8,128)S(1)}, f32[2,16,1,128]{3,1,2,0:T(8,128)S(1)}, u32[]{:S(2)}, u32[]{:S(2)}) collective-permute-start(f32[2,16,1,128]{3,1,2,0:T(8,128)S(1)} %get-tuple-element.69), channel_id=1, source_target_pairs={{64,0},{128,64},{192,128},{256,192},{320,256},{384,320},{448,384},... | collective-permute-start | bytes 49160 | tf_op jit(solution)/shard_map/ppermute | solution.py:17
  90.2 9.1 %collective-permute-start.14 = (f32[2,16,18,1]{3,1,2,0:T(8,128)S(1)}, f32[2,16,18,1]{3,1,2,0:T(8,128)S(1)}, u32[]{:S(2)}, u32[]{:S(2)}) collective-permute-start(f32[2,16,18,1]{3,1,2,0:T(8,128)S(1)} %get-tuple-element.48), channel_id=1, source_target_pairs={{0,16},{16,32},{32,48},{1,17},{17,33},{33,49},{2,18},{18,34},{34,5... | collective-permute-start | bytes 6920 | tf_op jit(solution)/shard_map/ppermute | solution.py:16
  91.5 9.2 %collective-permute-start.15 = (f32[2,16,18,1]{3,1,2,0:T(8,128)S(1)}, f32[2,16,18,1]{3,1,2,0:T(8,128)S(1)}, u32[]{:S(2)}, u32[]{:S(2)}) collective-permute-start(f32[2,16,18,1]{3,1,2,0:T(8,128)S(1)} %get-tuple-element.49), channel_id=1, source_target_pairs={{16,0},{32,16},{48,32},{17,1},{33,17},{49,33},{18,2},{34,18},{50,3... | collective-permute-start | bytes 6920 | tf_op jit(solution)/shard_map/ppermute | solution.py:17
  101.4 11.6 %collective-permute-start.16 = (f32[2,16,1,128]{3,1,2,0:T(8,128)S(1)}, f32[2,16,1,128]{3,1,2,0:T(8,128)S(1)}, u32[]{:S(2)}, u32[]{:S(2)}) collective-permute-start(f32[2,16,1,128]{3,1,2,0:T(8,128)S(1)} %get-tuple-element.66), channel_id=1, source_target_pairs={{0,64},{64,128},{128,192},{192,256},{256,320},{320,384},{384,448},... | collective-permute-start | bytes 49160 | tf_op jit(solution)/shard_map/ppermute | solution.py:16
  103.3 11.1 %collective-permute-start.17 = (f32[2,16,1,128]{3,1,2,0:T(8,128)S(1)}, f32[2,16,1,128]{3,1,2,0:T(8,128)S(1)}, u32[]{:S(2)}, u32[]{:S(2)}) collective-permute-start(f32[2,16,1,128]{3,1,2,0:T(8,128)S(1)} %get-tuple-element.67), channel_id=1, source_target_pairs={{64,0},{128,64},{192,128},{256,192},{320,256},{384,320},{448,384},... | collective-permute-start | bytes 49160 | tf_op jit(solution)/shard_map/ppermute | solution.py:17
  114.6 9.1 %collective-permute-start.18 = (f32[2,16,18,1]{3,1,2,0:T(8,128)S(1)}, f32[2,16,18,1]{3,1,2,0:T(8,128)S(1)}, u32[]{:S(2)}, u32[]{:S(2)}) collective-permute-start(f32[2,16,18,1]{3,1,2,0:T(8,128)S(1)} %get-tuple-element.44), channel_id=1, source_target_pairs={{0,16},{16,32},{32,48},{1,17},{17,33},{33,49},{2,18},{18,34},{34,5... | collective-permute-start | bytes 6920 | tf_op jit(solution)/shard_map/ppermute | solution.py:16
  115.9 9.2 %collective-permute-start.19 = (f32[2,16,18,1]{3,1,2,0:T(8,128)S(1)}, f32[2,16,18,1]{3,1,2,0:T(8,128)S(1)}, u32[]{:S(2)}, u32[]{:S(2)}) collective-permute-start(f32[2,16,18,1]{3,1,2,0:T(8,128)S(1)} %get-tuple-element.45), channel_id=1, source_target_pairs={{16,0},{32,16},{48,32},{17,1},{33,17},{49,33},{18,2},{34,18},{50,3... | collective-permute-start | bytes 6920 | tf_op jit(solution)/shard_map/ppermute | solution.py:17
  125.8 11.6 %collective-permute-start.20 = (f32[2,16,1,128]{3,1,2,0:T(8,128)S(1)}, f32[2,16,1,128]{3,1,2,0:T(8,128)S(1)}, u32[]{:S(2)}, u32[]{:S(2)}) collective-permute-start(f32[2,16,1,128]{3,1,2,0:T(8,128)S(1)} %get-tuple-element.64), channel_id=1, source_target_pairs={{0,64},{64,128},{128,192},{192,256},{256,320},{320,384},{384,448},... | collective-permute-start | bytes 49160 | tf_op jit(solution)/shard_map/ppermute | solution.py:16
  127.7 11.1 %collective-permute-start.21 = (f32[2,16,1,128]{3,1,2,0:T(8,128)S(1)}, f32[2,16,1,128]{3,1,2,0:T(8,128)S(1)}, u32[]{:S(2)}, u32[]{:S(2)}) collective-permute-start(f32[2,16,1,128]{3,1,2,0:T(8,128)S(1)} %get-tuple-element.65), channel_id=1, source_target_pairs={{64,0},{128,64},{192,128},{256,192},{320,256},{384,320},{448,384},... | collective-permute-start | bytes 49160 | tf_op jit(solution)/shard_map/ppermute | solution.py:17
  138.9 9.1 %collective-permute-start.22 = (f32[2,16,18,1]{3,1,2,0:T(8,128)S(1)}, f32[2,16,18,1]{3,1,2,0:T(8,128)S(1)}, u32[]{:S(2)}, u32[]{:S(2)}) collective-permute-start(f32[2,16,18,1]{3,1,2,0:T(8,128)S(1)} %get-tuple-element.40), channel_id=1, source_target_pairs={{0,16},{16,32},{32,48},{1,17},{17,33},{33,49},{2,18},{18,34},{34,5... | collective-permute-start | bytes 6920 | tf_op jit(solution)/shard_map/ppermute | solution.py:16
  140.2 9.2 %collective-permute-start.23 = (f32[2,16,18,1]{3,1,2,0:T(8,128)S(1)}, f32[2,16,18,1]{3,1,2,0:T(8,128)S(1)}, u32[]{:S(2)}, u32[]{:S(2)}) collective-permute-start(f32[2,16,18,1]{3,1,2,0:T(8,128)S(1)} %get-tuple-element.41), channel_id=1, source_target_pairs={{16,0},{32,16},{48,32},{17,1},{33,17},{49,33},{18,2},{34,18},{50,3... | collective-permute-start | bytes 6920 | tf_op jit(solution)/shard_map/ppermute | solution.py:17
  150.1 11.6 %collective-permute-start.24 = (f32[2,16,1,128]{3,1,2,0:T(8,128)S(1)}, f32[2,16,1,128]{3,1,2,0:T(8,128)S(1)}, u32[]{:S(2)}, u32[]{:S(2)}) collective-permute-start(f32[2,16,1,128]{3,1,2,0:T(8,128)S(1)} %get-tuple-element.62), channel_id=1, source_target_pairs={{0,64},{64,128},{128,192},{192,256},{256,320},{320,384},{384,448},... | collective-permute-start | bytes 49160 | tf_op jit(solution)/shard_map/ppermute | solution.py:16
  152.1 11.1 %collective-permute-start.25 = (f32[2,16,1,128]{3,1,2,0:T(8,128)S(1)}, f32[2,16,1,128]{3,1,2,0:T(8,128)S(1)}, u32[]{:S(2)}, u32[]{:S(2)}) collective-permute-start(f32[2,16,1,128]{3,1,2,0:T(8,128)S(1)} %get-tuple-element.63), channel_id=1, source_target_pairs={{64,0},{128,64},{192,128},{256,192},{320,256},{384,320},{448,384},... | collective-permute-start | bytes 49160 | tf_op jit(solution)/shard_map/ppermute | solution.py:17
  163.3 9.1 %collective-permute-start.26 = (f32[2,16,18,1]{3,1,2,0:T(8,128)S(1)}, f32[2,16,18,1]{3,1,2,0:T(8,128)S(1)}, u32[]{:S(2)}, u32[]{:S(2)}) collective-permute-start(f32[2,16,18,1]{3,1,2,0:T(8,128)S(1)} %get-tuple-element.36), channel_id=1, source_target_pairs={{0,16},{16,32},{32,48},{1,17},{17,33},{33,49},{2,18},{18,34},{34,5... | collective-permute-start | bytes 6920 | tf_op jit(solution)/shard_map/ppermute | solution.py:16
  164.6 9.2 %collective-permute-start.27 = (f32[2,16,18,1]{3,1,2,0:T(8,128)S(1)}, f32[2,16,18,1]{3,1,2,0:T(8,128)S(1)}, u32[]{:S(2)}, u32[]{:S(2)}) collective-permute-start(f32[2,16,18,1]{3,1,2,0:T(8,128)S(1)} %get-tuple-element.37), channel_id=1, source_target_pairs={{16,0},{32,16},{48,32},{17,1},{33,17},{49,33},{18,2},{34,18},{50,3... | collective-permute-start | bytes 6920 | tf_op jit(solution)/shard_map/ppermute | solution.py:17
  174.5 11.6 %collective-permute-start.28 = (f32[2,16,1,128]{3,1,2,0:T(8,128)S(1)}, f32[2,16,1,128]{3,1,2,0:T(8,128)S(1)}, u32[]{:S(2)}, u32[]{:S(2)}) collective-permute-start(f32[2,16,1,128]{3,1,2,0:T(8,128)S(1)} %get-tuple-element.60), channel_id=1, source_target_pairs={{0,64},{64,128},{128,192},{192,256},{256,320},{320,384},{384,448},... | collective-permute-start | bytes 49160 | tf_op jit(solution)/shard_map/ppermute | solution.py:16
  176.5 11.1 %collective-permute-start.29 = (f32[2,16,1,128]{3,1,2,0:T(8,128)S(1)}, f32[2,16,1,128]{3,1,2,0:T(8,128)S(1)}, u32[]{:S(2)}, u32[]{:S(2)}) collective-permute-start(f32[2,16,1,128]{3,1,2,0:T(8,128)S(1)} %get-tuple-element.61), channel_id=1, source_target_pairs={{64,0},{128,64},{192,128},{256,192},{320,256},{384,320},{448,384},... | collective-permute-start | bytes 49160 | tf_op jit(solution)/shard_map/ppermute | solution.py:17
  187.7 9.1 %collective-permute-start.30 = (f32[2,16,18,1]{3,1,2,0:T(8,128)S(1)}, f32[2,16,18,1]{3,1,2,0:T(8,128)S(1)}, u32[]{:S(2)}, u32[]{:S(2)}) collective-permute-start(f32[2,16,18,1]{3,1,2,0:T(8,128)S(1)} %get-tuple-element.32), channel_id=1, source_target_pairs={{0,16},{16,32},{32,48},{1,17},{17,33},{33,49},{2,18},{18,34},{34,5... | collective-permute-start | bytes 6920 | tf_op jit(solution)/shard_map/ppermute | solution.py:16
  189.0 29.5 %copy-start.2 = (f32[9]{0:T(128)S(1)}, f32[9]{0:T(128)}, u32[]{:S(2)}) copy-start(f32[9]{0:T(128)} %param.11) | copy-start | bytes 112
  189.0 9.2 %collective-permute-start.31 = (f32[2,16,18,1]{3,1,2,0:T(8,128)S(1)}, f32[2,16,18,1]{3,1,2,0:T(8,128)S(1)}, u32[]{:S(2)}, u32[]{:S(2)}) collective-permute-start(f32[2,16,18,1]{3,1,2,0:T(8,128)S(1)} %get-tuple-element.33), channel_id=1, source_target_pairs={{16,0},{32,16},{48,32},{17,1},{33,17},{49,33},{18,2},{34,18},{50,3... | collective-permute-start | bytes 6920 | tf_op jit(solution)/shard_map/ppermute | solution.py:17
  198.7 24.4 %copy-start.1 = (f32[16,16,128]{2,1,0:T(8,128)S(1)}, f32[16,16,128]{2,1,0:T(8,128)}, u32[]{:S(2)}) copy-start(f32[16,16,128]{2,1,0:T(8,128)} %param.6) | copy-start | bytes 393220
  198.9 11.6 %collective-permute-start.32 = (f32[2,16,1,128]{3,1,2,0:T(8,128)S(1)}, f32[2,16,1,128]{3,1,2,0:T(8,128)S(1)}, u32[]{:S(2)}, u32[]{:S(2)}) collective-permute-start(f32[2,16,1,128]{3,1,2,0:T(8,128)S(1)} %get-tuple-element.58), channel_id=1, source_target_pairs={{0,64},{64,128},{128,192},{192,256},{256,320},{320,384},{384,448},... | collective-permute-start | bytes 49160 | tf_op jit(solution)/shard_map/ppermute | solution.py:16
  200.9 11.1 %collective-permute-start.33 = (f32[2,16,1,128]{3,1,2,0:T(8,128)S(1)}, f32[2,16,1,128]{3,1,2,0:T(8,128)S(1)}, u32[]{:S(2)}, u32[]{:S(2)}) collective-permute-start(f32[2,16,1,128]{3,1,2,0:T(8,128)S(1)} %get-tuple-element.59), channel_id=1, source_target_pairs={{64,0},{128,64},{192,128},{256,192},{320,256},{384,320},{448,384},... | collective-permute-start | bytes 49160 | tf_op jit(solution)/shard_map/ppermute | solution.py:17
  212.1 9.1 %collective-permute-start.34 = (f32[2,16,18,1]{3,1,2,0:T(8,128)S(1)}, f32[2,16,18,1]{3,1,2,0:T(8,128)S(1)}, u32[]{:S(2)}, u32[]{:S(2)}) collective-permute-start(f32[2,16,18,1]{3,1,2,0:T(8,128)S(1)} %get-tuple-element.28), channel_id=1, source_target_pairs={{0,16},{16,32},{32,48},{1,17},{17,33},{33,49},{2,18},{18,34},{34,5... | collective-permute-start | bytes 6920 | tf_op jit(solution)/shard_map/ppermute | solution.py:16
  213.4 9.2 %collective-permute-start.35 = (f32[2,16,18,1]{3,1,2,0:T(8,128)S(1)}, f32[2,16,18,1]{3,1,2,0:T(8,128)S(1)}, u32[]{:S(2)}, u32[]{:S(2)}) collective-permute-start(f32[2,16,18,1]{3,1,2,0:T(8,128)S(1)} %get-tuple-element.29), channel_id=1, source_target_pairs={{16,0},{32,16},{48,32},{17,1},{33,17},{49,33},{18,2},{34,18},{50,3... | collective-permute-start | bytes 6920 | tf_op jit(solution)/shard_map/ppermute | solution.py:17
  229.6 298.1 %all-reduce.3.cloned.1.call-start = ((), (), s32[]{:S(2)}) async-start(), calls=%async_computation.1 | async-start | bytes 1572864
Sparse Core Ops, SparseCore 0:
  229.8 84.9 all-gather.1
  318.2 209.4 all-reduce.2
where the time goes:
time: 541 us; the launch traced here: 536 us
  waiting for transfers between devices  336 us (62%)
  starting transfers between devices  161 us (30%)
  between operations  15.4 us (3%)
  other arithmetic  13.4 us (2%)
  local copies, waits for them, and re-layouts  7.7 us (1%)
    unnamed x3, waiting for transfers between devices  207 us
    ppermute x18, starting transfers between devices, padded(): after = lax.ppermute(first, axis, down)  132 us
    all_gather x1, waiting for transfers between devices, on_device(): piece = lax.all_gather(lowered, 'cr', axis=0, tiled=True)  85.1 us
    ppermute x18, starting transfers between devices, padded(): before = lax.ppermute(last, axis, up)  29 us
    ppermute x18, waiting for transfers between devices, padded(): after = lax.ppermute(first, axis, down)  23 us
    ppermute x18, waiting for transfers between devices, padded(): before = lax.ppermute(last, axis, up)  20.3 us
  transfers between devices with their start and end apart: 38, of which 26 were waited for; matrix products, arithmetic and copies ran while one was open for 1% of the time, Pallas kernels for 0%

commit v1 on v0

v1 whole, which is shorter than its diff:
```python
import functools

import jax
import jax.numpy as jnp
from jax import lax
from jax.experimental import pallas as pl
from jax.experimental.pallas import tpu as pltpu
from jax.sharding import PartitionSpec as P

DEG = 8
LANES = 128
HALF = LANES // 2
PIECES = 2
MESH = pl.DeviceIdType.MESH


def lane_iota(shape):
    return lax.broadcasted_iota(jnp.int32, shape, len(shape) - 1)


def roll(value, shift):
    return pltpu.roll(value, shift % LANES, value.ndim - 1)


def lookup(ids, table):
    out = jnp.zeros(ids.shape, jnp.float32)
    for material in range(table.shape[0]):
        out = jnp.where(ids == material, table[material], out)
    return out


def load_own(wide, scaled, main, acc, coef):
    nx = scaled.shape[1]
    for x in range(nx):
        for g in range(2):
            value = wide[pl.ds(g * 8 * nx + x, 8, stride=nx), :]
            if g == 1:
                value = roll(value, HALF)
            value = scaled[g, x] * value
            main[0, DEG + x, g] = value
            acc[x, g] = coef[0] * value


def pack_edges(main, packed, nx):
    lane = lane_iota((8, LANES))
    window = lax.rem(lane, HALF) // DEG
    low = lane < HALF
    for xb in range(nx // 8):
        first = jnp.zeros((8, LANES), jnp.float32)
        last = jnp.zeros((8, LANES), jnp.float32)
        for i in range(8):
            m0 = main[0, DEG + 8 * xb + i, 0]
            m1 = main[0, DEG + 8 * xb + i, 1]
            first = jnp.where(window == i, roll(jnp.where(low, m0, m1), 8 * i), first)
            last = jnp.where(window == i, roll(jnp.where(low, m1, m0), 8 * (i + 1)), last)
        packed[0, xb] = first
        packed[1, xb] = last


def unpack_edges(got, side):
    lane = lax.rem(lane_iota((8, LANES)), HALF)
    for xb in range(got.shape[1]):
        left = got[0, xb]
        right = got[1, xb]
        for i in range(8):
            value = jnp.where(lane >= HALF - DEG, roll(left, -8 * (i + 1)), 0.0)
            side[0, 8 * xb + i] = jnp.where(lane < DEG, roll(right, -8 * i), value)


def build_fields(ids, mat_diag, mat_cond, diag2, cond2):
    middle = ids[1]
    rows = middle.shape[0]
    lane = lane_iota((rows, LANES))
    in_half = lax.rem(lane, HALF)
    lower = lane < HALF
    left = jnp.where(lower, roll(ids[0], HALF), ids[0])
    right = jnp.where(lower, ids[2], roll(ids[2], HALF))
    edges = jnp.where(in_half < DEG, right, jnp.where(in_half >= HALF - DEG, left, -1))
    for t, tile in enumerate((middle, None, edges)):
        if tile is None:
            d, c = roll(diag, HALF), roll(cond, HALF)
        else:
            diag, cond = lookup(tile, mat_diag), lookup(tile, mat_cond)
            d, c = diag, cond
        diag2[t] = jnp.broadcast_to((2.0 * d)[:, None, :], (rows, 8, LANES))
        cond2[t] = jnp.broadcast_to((2.0 * c * c)[:, None, :], (rows, 8, LANES))


def own_cond(ids_ref, mat_cond, scaled, unscaled):
    cond = lookup(ids_ref[...], mat_cond)
    nx = cond.shape[0]
    for g in range(2):
        value = cond if g == 0 else roll(cond, HALF)
        scaled[g] = jnp.broadcast_to(value[:, None, :], (nx, 8, LANES))
        unscaled[g] = jnp.broadcast_to((1.0 / value)[:, None, :], (nx, 8, LANES))


def filter_steps(main, side, diag2, cond2, acc, coef, nx):
    rows = nx + 2 * DEG
    for k in range(1, DEG + 1):
        cur, new = (k + 1) % 2, k % 2
        cuts = [k] + [c for c in range(8, rows, 8) if k < c < rows - k] + [rows - k]
        for a, b in zip(cuts[:-1], cuts[1:]):
            lane = lane_iota((b - a, 8, LANES))
            whole = [main[cur, a - 1 : b + 1, 0], main[cur, a - 1 : b + 1, 1], side[cur, a - 1 : b + 1]]
            middle = [w[1:-1] for w in whole]
            before = [roll(m, 1) for m in middle]
            after = [roll(m, -1) for m in middle]
            wrap_b = (0, HALF)
            wrap_a = (LANES - 1, HALF - 1)
            for t in range(3 if k < DEG else 2):
                if t < 2:
                    lhs = jnp.where(lane == wrap_b[t], before[2], before[t])
                    rhs = jnp.where(lane == wrap_a[t], after[2], after[t])
                else:
                    lhs = jnp.where(lane == wrap_b[0], before[0], jnp.where(lane == wrap_b[1], before[1], before[2]))
                    rhs = jnp.where(lane == wrap_a[0], after[0], jnp.where(lane == wrap_a[1], after[1], after[2]))
                beside = (whole[t][:-2] + whole[t][2:]) + (lhs + rhs)
                value = diag2[t, a:b] * middle[t] + cond2[t, a:b] * beside
                if k == 1:
                    value = 0.5 * value
                elif t < 2:
                    value = value - main[new, a:b, t]
                else:
                    value = value - side[new, a:b]
                if t == 2:
                    side[new, a:b] = value
                else:
                    if k < DEG:
                        main[new, a:b, t] = value
                    if a >= DEG and b <= rows - DEG:
                        acc[a - DEG : b - DEG, t] = acc[a - DEG : b - DEG, t] + coef[k] * value


def finish(acc, unscaled, smooth, cols, nx):
    depth = cols.shape[-1]
    for x in range(nx):
        done = []
        for g in range(2):
            value = acc[x, g] * unscaled[g, x]
            if g == 1:
                value = roll(value, HALF)
            smooth[pl.ds(g * 8 * nx + x, 8, stride=nx), :] = value
            done.append(value)
        at = x * LANES
        cols[at // depth, 0, :, at % depth : at % depth + LANES] = jnp.concatenate(done, axis=0).astype(jnp.bfloat16)


def turn_rows(raw, flat):
    step = 16
    nx = raw.shape[1]

    def body(i, carry):
        at = pl.ds(pl.multiple_of(i * step, step), step)
        turned = jnp.swapaxes(raw[at], 0, 1)
        for x in range(nx):
            flat[at, x * LANES : (x + 1) * LANES] = turned[x]
        return carry

    lax.fori_loop(0, raw.shape[0] // step, body, 0)


def kernel(
    sizes,
    adj_hbm, rows_hbm, ids_ref, mat_diag, mat_cond, coef,
    smooth_hbm, panel_ref,
    wide, raw, flat, ids, scaled, unscaled, main, side, acc, packed, got, diag2, cond2, smooth, cols,
    out_a, in_a, out_b, in_b,
    local_sem, halo_send, halo_recv, z_send, z_recv, a_send, a_recv, b_send, b_recv,
):
    nsx, nsy, ncr = sizes
    low = nsx // 2
    me_x, me_y, me_z = lax.axis_index("sx"), lax.axis_index("sy"), lax.axis_index("cr")
    me_low, me_high = lax.rem(me_x, low), me_x // low
    nx = ids_ref.shape[0]
    nc = out_a.shape[1]
    steps = ncr // 2
    load_adj = pltpu.make_async_copy(adj_hbm, wide, local_sem.at[0])
    load_rows = pltpu.make_async_copy(rows_hbm, raw, local_sem.at[1])
    load_adj.start()
    load_rows.start()

    sides = []
    for dx in (-1, 0, 1):
        for dy in (-1, 0, 1):
            if dx or dy:
                x, y = me_x + dx, me_y + dy
                sides.append((dx, dy, (x >= 0) & (x < nsx) & (y >= 0) & (y < nsy), (x, y, me_z)))
    up = (me_x, me_y, lax.rem(me_z + 1, ncr))
    down = (me_x, me_y, lax.rem(me_z + ncr - 1, ncr))

    barrier = pltpu.get_barrier_semaphore()

    def greet(*device):
        pl.semaphore_signal(barrier, inc=1, device_id=device, device_id_type=MESH)

    greet(*up)
    greet(*down)
    for q in range(low):
        pl.when(q != me_low)(functools.partial(greet, me_high * low + q, me_y, me_z))
    for h in range(2):
        for y in range(nsy):
            pl.when((h != me_high) | (y != me_y))(functools.partial(greet, h * low + me_low, y, me_z))
    for dx in (-1, 1):
        for dy in (-1, 1):
            greet(lax.rem(me_x + nsx + dx, nsx), lax.rem(me_y + nsy + dy, nsy), me_z)
    first_low, last_low = me_low == 0, me_low == low - 1
    pl.when(first_low)(functools.partial(greet, lax.rem(me_x + nsx - 1, nsx), me_y, me_z))
    pl.when(last_low)(functools.partial(greet, lax.rem(me_x + 1, nsx), me_y, me_z))
    peers = 2 + (low - 1) + (2 * nsy - 1) + 4

    own_cond(ids_ref, mat_cond, scaled, unscaled)
    ids[1, DEG : DEG + nx] = ids_ref[...]
    load_adj.wait()
    load_own(wide, scaled, main, acc, coef)
    pack_edges(main, packed, nx)

    @pl.when(first_low | last_low)
    def _():
        pl.semaphore_wait(barrier, peers + 1)

    @pl.when(jnp.logical_not(first_low | last_low))
    def _():
        pl.semaphore_wait(barrier, peers)

    def rows_from(d):
        return {-1: (0, 8), 0: (0, nx), 1: (nx - 8, nx)}[d]

    def rows_to(d):
        return {-1: (DEG + nx, 2 * DEG + nx), 0: (DEG, DEG + nx), 1: (0, 8)}[d]

    halos = []
    for i, (dx, dy, there, device) in enumerate(sides):
        (a, b), (c, d) = rows_from(dx), rows_to(dx)
        if dy == 0:
            src = main.at[0, DEG + a : DEG + b]
            dst = main.at[0, c:d]
        else:
            src = packed.at[0 if dy < 0 else 1, a // 8 : b // 8]
            dst = got.at[1 if dy < 0 else 0, c // 8 : d // 8]
        halos.append((there, [
            pltpu.make_async_remote_copy(
                src_ref=src, dst_ref=dst, send_sem=halo_send.at[0, i], recv_sem=halo_recv.at[0, i],
                device_id=device, device_id_type=MESH),
            pltpu.make_async_remote_copy(
                src_ref=ids_ref.at[a:b], dst_ref=ids.at[1 - dy, c:d], send_sem=halo_send.at[1, i],
                recv_sem=halo_recv.at[1, i], device_id=device, device_id_type=MESH),
        ]))

    order = sorted(range(8), key=lambda i: abs(sides[i][1]))
    for i in order:
        there, copies = halos[i]

        @pl.when(there)
        def _(copies=copies):
            copies[0].start()
            copies[1].start()

    for i, (dx, dy, there, device) in enumerate(sides):
        c, d = rows_to(-dx)

        @pl.when(jnp.logical_not(there))
        def _(dx=dx, dy=dy, c=c, d=d):
            ids[1 + dy, c:d] = jnp.full((d - c, LANES), -1, jnp.int32)
            if dy == 0:
                main[0, c:d] = jnp.zeros((d - c, 2, 8, LANES), jnp.float32)
            else:
                got[0 if dy < 0 else 1, c // 8 : d // 8] = jnp.zeros(((d - c) // 8, 8, LANES), jnp.float32)

    load_rows.wait()
    turn_rows(raw, flat)

    for i, (dx, dy, there, device) in enumerate(sides):
        there_copies = halos[7 - i][1]

        @pl.when(there)
        def _(mine=halos[i][1], theirs=there_copies):
            for copy in mine:
                copy.wait_send()
            for copy in theirs:
                copy.wait_recv()

    build_fields(ids, mat_diag, mat_cond, diag2, cond2)
    unpack_edges(got, side)
    filter_steps(main, side, diag2, cond2, acc, coef, nx)
    finish(acc, unscaled, smooth, cols, nx)

    def hop(way, s, p):
        last = s == steps
        here = 0 if s == 1 else 2 * (s - 1) - 1 + way
        slot = 2 * s - 1 if last else 2 * s - 1 + way
        return pltpu.make_async_remote_copy(
            src_ref=cols.at[p, here], dst_ref=cols.at[p, slot], send_sem=z_send.at[way, s - 1, p],
            recv_sem=z_recv.at[way, s - 1, p], device_id=up if way == 0 else down, device_id_type=MESH)

    def hops(s):
        return [(way, p) for p in range(PIECES) for way in range(2)
                if s < steps or p % 2 == way]

    for way, p in hops(1):
        hop(way, 1, p).start()
    store = pltpu.make_async_copy(smooth, smooth_hbm, local_sem.at[2])
    store.start()

    def arrive(s):
        for way, p in hops(s):
            hop(way, s, p).wait_recv()
            if s < steps and (way, p) in hops(s + 1):
                hop(way, s + 1, p).start()

    def block_of(slot):
        s = (slot + 1) // 2
        return lax.rem(me_z + ncr - s, ncr) if slot % 2 else lax.rem(me_z + s, ncr)

    def multiply(first, last, half):
        count = (last - first) * nc
        wide_rows = flat.shape[0] // 2
        depth = cols.shape[-1]
        total = None
        for p in range(PIECES):
            lhs = cols[p, first:last].reshape(count, depth)
            rhs = flat[half * wide_rows : (half + 1) * wide_rows, p * depth : (p + 1) * depth]
            part = lax.dot_general(lhs, rhs, (((1,), (1,)), ((), ())), preferred_element_type=jnp.float32)
            total = part if total is None else total + part
        out_a[first:last, :, half * wide_rows : (half + 1) * wide_rows] = total.astype(jnp.bfloat16).reshape(
            last - first, nc, wide_rows)

    def send_a(slot):
        block = block_of(slot)
        to_low, high = lax.rem(block, low), block // low
        return to_low, high, pltpu.make_async_remote_copy(
            src_ref=out_a.at[slot], dst_ref=in_a.at[high, me_low], send_sem=a_send.at[slot],
            recv_sem=a_recv.at[high, me_low], device_id=(me_high * low + to_low, me_y, me_z), device_id_type=MESH)

    def share(first, last):
        for slot in range(first, last):
            to_low, high, copy = send_a(slot)
            pl.when(to_low != me_low)(copy.start)

            @pl.when(to_low == me_low)
            def _(slot=slot, high=high):
                in_a[high, me_low] = out_a[slot]

    def send_b(h, y):
        return pltpu.make_async_remote_copy(
            src_ref=out_b.at[h, y], dst_ref=in_b.at[me_high * nsy + me_y], send_sem=b_send.at[h, y],
            recv_sem=b_recv.at[me_high * nsy + me_y], device_id=(h * low + me_low, y, me_z), device_id_type=MESH)

    def gather_a(h):
        for q in range(low):
            @pl.when(q != me_low)
            def _(q=q):
                pltpu.make_async_remote_copy(
                    src_ref=out_a.at[0], dst_ref=in_a.at[h, q], send_sem=a_send.at[0],
                    recv_sem=a_recv.at[h, q], device_id=(me_high * low + q, me_y, me_z),
                    device_id_type=MESH).wait_recv()
        total = in_a[h, 0].astype(jnp.float32)
        for q in range(1, low):
            total = total + in_a[h, q].astype(jnp.float32)
        oc = nc // nsy
        for y in range(nsy):
            out_b[h, y] = total[y * oc : (y + 1) * oc]
        for y in range(nsy):
            mine = (h == me_high) & (y == me_y)
            pl.when(jnp.logical_not(mine))(send_b(h, y).start)

            @pl.when(mine)
            def _(y=y):
                in_b[me_high * nsy + me_y] = out_b[h, y]

    early = lax.rem(me_low - me_z + ncr + ncr // 4, ncr) // (ncr // 2 + 1)

    groups = []
    s = steps
    while s > 0:
        before = max(s - 2, 0)
        groups.append((before, s))
        s = before
    groups.reverse()
    for n, (before, last_step) in enumerate(groups):
        first = 0 if before == 0 else 2 * before + 1
        last = 2 * last_step + 1 if last_step < steps else 2 * steps
        arrive(before + 1)
        if n:
            multiply(pending[0], pending[1], 0)
        if before + 2 <= last_step:
            arrive(before + 2)
        if n:
            multiply(pending[0], pending[1], 1)
            share(pending[0], pending[1])
        pending = (first, last)
    gather_a(early)
    multiply(pending[0], pending[1], 0)
    multiply(pending[0], pending[1], 1)
    share(pending[0], pending[1])
    gather_a(1 - early)
    for peer in range(2 * nsy):
        h, y = peer // nsy, peer % nsy

        @pl.when((h != me_high) | (y != me_y))
        def _(peer=peer, h=h, y=y):
            pltpu.make_async_remote_copy(
                src_ref=out_b.at[0, 0], dst_ref=in_b.at[peer], send_sem=b_send.at[0, 0],
                recv_sem=b_recv.at[peer], device_id=(h * low + me_low, y, me_z), device_id_type=MESH).wait_recv()
    total = in_b[0]
    for peer in range(1, 2 * nsy):
        total = total + in_b[peer]
    panel_ref[...] = total

    for s in range(1, steps + 1):
        for way, p in hops(s):
            hop(way, s, p).wait_send()
    for slot in range(2 * steps):
        to_low, high, copy = send_a(slot)
        pl.when(to_low != me_low)(copy.wait_send)
    for h in range(2):
        for y in range(nsy):
            pl.when((h != me_high) | (y != me_y))(send_b(h, y).wait_send)
    store.wait()


def on_device(sizes, adjoint, sensor_rows, cell_ids, mat_diag, mat_cond, cheb_coef):
    nsx, nsy, ncr = sizes
    nc, nx, ny = adjoint.shape
    nr = sensor_rows.shape[0]
    low = nsx // 2
    wide = nx + 2 * DEG
    oc = nc // nsy
    f32, bf16 = jnp.float32, jnp.bfloat16
    vmem = pl.BlockSpec(memory_space=pltpu.VMEM)
    smem = pl.BlockSpec(memory_space=pltpu.SMEM)
    hbm = pl.BlockSpec(memory_space=pl.ANY)
    dma = pltpu.SemaphoreType.DMA
    smooth, panel = pl.pallas_call(
        functools.partial(kernel, sizes),
        out_shape=(jax.ShapeDtypeStruct((nc * nx, ny), f32), jax.ShapeDtypeStruct((oc, nr), f32)),
        in_specs=[hbm, hbm, vmem, smem, smem, smem],
        out_specs=(hbm, vmem),
        scratch_shapes=[
            pltpu.VMEM((nc * nx, ny), f32),
            pltpu.VMEM((nr, nx, ny), bf16),
            pltpu.VMEM((nr, nx * ny), bf16),
            pltpu.VMEM((3, wide, ny), jnp.int32),
            pltpu.VMEM((2, nx, 8, ny), f32),
            pltpu.VMEM((2, nx, 8, ny), f32),
            pltpu.VMEM((2, wide, 2, 8, ny), f32),
            pltpu.VMEM((2, wide, 8, ny), f32),
            pltpu.VMEM((nx, 2, 8, ny), f32),
            pltpu.VMEM((2, nx // 8, 8, ny), f32),
            pltpu.VMEM((2, wide // 8, 8, ny), f32),
            pltpu.VMEM((3, wide, 8, ny), f32),
            pltpu.VMEM((3, wide, 8, ny), f32),
            pltpu.VMEM((nc * nx, ny), f32),
            pltpu.VMEM((PIECES, ncr, nc, nx * ny // PIECES), bf16),
            pltpu.VMEM((ncr, nc, nr), bf16),
            pltpu.VMEM((2, low, nc, nr), bf16),
            pltpu.VMEM((2, nsy, oc, nr), f32),
            pltpu.VMEM((2 * nsy, oc, nr), f32),
            dma((3,)),
            dma((2, 8)),
            dma((2, 8)),
            dma((2, ncr // 2, PIECES)),
            dma((2, ncr // 2, PIECES)),
            dma((ncr,)),
            dma((2, low)),
            dma((2, nsy)),
            dma((2 * nsy,)),
        ],
        compiler_params=pltpu.CompilerParams(
            collective_id=0, has_side_effects=True, vmem_limit_bytes=62 << 20
        ),
    )(adjoint.reshape(nc * nx, ny), sensor_rows, cell_ids, mat_diag, mat_cond, cheb_coef)
    return smooth.reshape(nc, nx, ny), panel.T


def solution(mesh):
    placed = (P("cr", "sx", "sy"), P("cr", "sx", "sy"), P("sx", "sy"), P(), P(), P())
    sizes = tuple(mesh.shape[axis] for axis in ("sx", "sy", "cr"))
    return jax.shard_map(
        functools.partial(on_device, sizes),
        mesh=mesh,
        in_specs=placed,
        out_specs=(P("cr", "sx", "sy"), P("cr", ("sx", "sy"))),
        check_vma=False,
    )
```

time: 541 us -> 70.2 us (0.13)
  the two profiles are of different devices: /device:TPU:56 before, /device:TPU:15 now
where the time goes in v1:
time: 70.2 us; the launch traced here: 70 us
  Pallas kernels  66.5 us (95%)
  local copies, waits for them, and re-layouts  2.87 us (4%)
    pallas_call x1, Pallas kernels, on_device(): pl.pallas_call(functools.partial(kernel, sizes), out_shape=(jax.ShapeDtyp...  66.5 us
    unnamed x2, local copies, waits for them, and re-layouts  2.87 us

profile of v1, /device:TPU:15, one launch (start us, length us, event | category | flops | bytes accessed | tf_op | source)
XLA Modules:
  0.0 70.0 jit_solution(6937449741236486844)
XLA Ops:
  0.6 66.5 %shard_map.77 = (f32[256,128]{1,0:T(8,128)}, f32[4,768]{1,0:T(4,128)}) custom-call(f32[256,128]{1,0:T(8,128)} %bitcast.3, bf16[768,16,128]{2,1,0:T(8,128)(2,1)} %rows_hbm.1, s32[16,128]{1,0:T(8,128)} %ids_ref.1, f32[16]{0:T(128)} %mat_diag.1, f32[16]{0:T(128)} %mat_cond.1, f32[9]{0:T(128)} %coef.1), custom_call_target="tpu_custom_call" | custom-call | tf_op jit(solution)/shard_map/pallas_call | solution.py:434
  67.1 1.6 %copy.10 = f32[16,16,128]{2,1,0:T(8,128)} copy(f32[16,16,128]{2,1,0:T(8,128)} %bitcast.4) | data formatting | bytes 262144
  68.7 1.3 %copy.11 = f32[768,4]{0,1:T(4,128)} copy(f32[768,4]{0,1:T(4,128)} %bitcast.5) | data formatting | bytes 24576

commit v2 on v1

--- a/solution.py
+++ b/solution.py
@@ -55,6 +55,18 @@
             last = jnp.where(window == i, roll(jnp.where(low, m1, m0), 8 * (i + 1)), last)
         packed[0, xb] = first
         packed[1, xb] = last
+
+
+def thin_edges(main, thin, nx):
+    for e, start in enumerate((DEG, nx)):
+        for x in range(8):
+            thin[e, x] = main[0, start + x].reshape(16, LANES).astype(jnp.bfloat16)
+
+
+def widen_edges(thin_got, main, nx):
+    for e, start in enumerate((0, DEG + nx)):
+        for x in range(8):
+            main[0, start + x] = thin_got[e, x].astype(jnp.float32).reshape(2, 8, LANES)
 
 
 def unpack_edges(got, side):
@@ -163,8 +175,8 @@
 def kernel(
     sizes,
     adj_hbm, rows_hbm, ids_ref, mat_diag, mat_cond, coef,
-    smooth_hbm, panel_ref,
-    wide, raw, flat, ids, scaled, unscaled, main, side, acc, packed, got, diag2, cond2, smooth, cols,
+    smooth, panel_ref,
+    wide, raw, flat, ids, scaled, unscaled, main, side, acc, packed, got, thin, thin_got, diag2, cond2, cols,
     out_a, in_a, out_b, in_b,
     local_sem, halo_send, halo_recv, z_send, z_recv, a_send, a_recv, b_send, b_recv,
 ):
@@ -214,6 +226,7 @@
     load_adj.wait()
     load_own(wide, scaled, main, acc, coef)
     pack_edges(main, packed, nx)
+    thin_edges(main, thin, nx)
 
     @pl.when(first_low | last_low)
     def _():
@@ -233,8 +246,8 @@
     for i, (dx, dy, there, device) in enumerate(sides):
         (a, b), (c, d) = rows_from(dx), rows_to(dx)
         if dy == 0:
-            src = main.at[0, DEG + a : DEG + b]
-            dst = main.at[0, c:d]
+            src = thin.at[0 if dx < 0 else 1]
+            dst = thin_got.at[1 if dx < 0 else 0]
         else:
             src = packed.at[0 if dy < 0 else 1, a // 8 : b // 8]
             dst = got.at[1 if dy < 0 else 0, c // 8 : d // 8]
@@ -263,12 +276,9 @@
         def _(dx=dx, dy=dy, c=c, d=d):
             ids[1 + dy, c:d] = jnp.full((d - c, LANES), -1, jnp.int32)
             if dy == 0:
-                main[0, c:d] = jnp.zeros((d - c, 2, 8, LANES), jnp.float32)
+                thin_got[0 if dx < 0 else 1] = jnp.zeros((8, 16, LANES), jnp.bfloat16)
             else:
                 got[0 if dy < 0 else 1, c // 8 : d // 8] = jnp.zeros(((d - c) // 8, 8, LANES), jnp.float32)
-
-    load_rows.wait()
-    turn_rows(raw, flat)
 
     for i, (dx, dy, there, device) in enumerate(sides):
         there_copies = halos[7 - i][1]
@@ -282,6 +292,7 @@
 
     build_fields(ids, mat_diag, mat_cond, diag2, cond2)
     unpack_edges(got, side)
+    widen_edges(thin_got, main, nx)
     filter_steps(main, side, diag2, cond2, acc, coef, nx)
     finish(acc, unscaled, smooth, cols, nx)
 
@@ -299,8 +310,8 @@
 
     for way, p in hops(1):
         hop(way, 1, p).start()
-    store = pltpu.make_async_copy(smooth, smooth_hbm, local_sem.at[2])
-    store.start()
+    load_rows.wait()
+    turn_rows(raw, flat)
 
     def arrive(s):
         for way, p in hops(s):
@@ -312,18 +323,16 @@
         s = (slot + 1) // 2
         return lax.rem(me_z + ncr - s, ncr) if slot % 2 else lax.rem(me_z + s, ncr)
 
-    def multiply(first, last, half):
+    def multiply(first, last):
         count = (last - first) * nc
-        wide_rows = flat.shape[0] // 2
         depth = cols.shape[-1]
         total = None
         for p in range(PIECES):
             lhs = cols[p, first:last].reshape(count, depth)
-            rhs = flat[half * wide_rows : (half + 1) * wide_rows, p * depth : (p + 1) * depth]
+            rhs = flat[:, p * depth : (p + 1) * depth]
             part = lax.dot_general(lhs, rhs, (((1,), (1,)), ((), ())), preferred_element_type=jnp.float32)
             total = part if total is None else total + part
-        out_a[first:last, :, half * wide_rows : (half + 1) * wide_rows] = total.astype(jnp.bfloat16).reshape(
-            last - first, nc, wide_rows)
+        out_a[first:last] = total.astype(jnp.bfloat16).reshape(last - first, nc, flat.shape[0])
 
     def send_a(slot):
         block = block_of(slot)
@@ -370,29 +379,14 @@
 
     early = lax.rem(me_low - me_z + ncr + ncr // 4, ncr) // (ncr // 2 + 1)
 
-    groups = []
-    s = steps
-    while s > 0:
-        before = max(s - 2, 0)
-        groups.append((before, s))
-        s = before
-    groups.reverse()
-    for n, (before, last_step) in enumerate(groups):
-        first = 0 if before == 0 else 2 * before + 1
-        last = 2 * last_step + 1 if last_step < steps else 2 * steps
-        arrive(before + 1)
-        if n:
-            multiply(pending[0], pending[1], 0)
-        if before + 2 <= last_step:
-            arrive(before + 2)
-        if n:
-            multiply(pending[0], pending[1], 1)
-            share(pending[0], pending[1])
-        pending = (first, last)
-    gather_a(early)
-    multiply(pending[0], pending[1], 0)
-    multiply(pending[0], pending[1], 1)
-    share(pending[0], pending[1])
+    for s in range(1, steps + 1):
+        first = 0 if s == 1 else 2 * s - 1
+        last = min(2 * s + 1, 2 * steps)
+        arrive(s)
+        multiply(first, last)
+        share(first, last)
+        if s == steps - 1:
+            gather_a(early)
     gather_a(1 - early)
     for peer in range(2 * nsy):
         h, y = peer // nsy, peer % nsy
@@ -416,7 +410,17 @@
     for h in range(2):
         for y in range(nsy):
             pl.when((h != me_high) | (y != me_y))(send_b(h, y).wait_send)
-    store.wait()
+
+
+def write_out(smooth, panel, smooth_out, panel_out, sem):
+    copies = [
+        pltpu.make_async_copy(smooth, smooth_out, sem.at[0]),
+        pltpu.make_async_copy(panel, panel_out, sem.at[1]),
+    ]
+    for copy in copies:
+        copy.start()
+    for copy in copies:
+        copy.wait()
 
 
 def on_device(sizes, adjoint, sensor_rows, cell_ids, mat_diag, mat_cond, cheb_coef):
@@ -435,7 +439,7 @@
         functools.partial(kernel, sizes),
         out_shape=(jax.ShapeDtypeStruct((nc * nx, ny), f32), jax.ShapeDtypeStruct((oc, nr), f32)),
         in_specs=[hbm, hbm, vmem, smem, smem, smem],
-        out_specs=(hbm, vmem),
+        out_specs=(vmem, vmem),
         scratch_shapes=[
             pltpu.VMEM((nc * nx, ny), f32),
             pltpu.VMEM((nr, nx, ny), bf16),
@@ -448,15 +452,16 @@
             pltpu.VMEM((nx, 2, 8, ny), f32),
             pltpu.VMEM((2, nx // 8, 8, ny), f32),
             pltpu.VMEM((2, wide // 8, 8, ny), f32),
+            pltpu.VMEM((2, 8, 16, ny), bf16),
+            pltpu.VMEM((2, 8, 16, ny), bf16),
             pltpu.VMEM((3, wide, 8, ny), f32),
             pltpu.VMEM((3, wide, 8, ny), f32),
-            pltpu.VMEM((nc * nx, ny), f32),
             pltpu.VMEM((PIECES, ncr, nc, nx * ny // PIECES), bf16),
             pltpu.VMEM((ncr, nc, nr), bf16),
             pltpu.VMEM((2, low, nc, nr), bf16),
             pltpu.VMEM((2, nsy, oc, nr), f32),
             pltpu.VMEM((2 * nsy, oc, nr), f32),
-            dma((3,)),
+            dma((2,)),
             dma((2, 8)),
             dma((2, 8)),
             dma((2, ncr // 2, PIECES)),
@@ -470,6 +475,13 @@
             collective_id=0, has_side_effects=True, vmem_limit_bytes=62 << 20
         ),
     )(adjoint.reshape(nc * nx, ny), sensor_rows, cell_ids, mat_diag, mat_cond, cheb_coef)
+    smooth, panel = pl.pallas_call(
+        write_out,
+        out_shape=(jax.ShapeDtypeStruct(smooth.shape, f32), jax.ShapeDtypeStruct(panel.shape, f32)),
+        in_specs=[vmem, vmem],
+        out_specs=(hbm, hbm),
+        scratch_shapes=[dma((2,))],
+    )(smooth, panel)
     return smooth.reshape(nc, nx, ny), panel.T
 
 

time: 70.2 us -> 65.4 us (0.932)
  the two profiles are of different devices: /device:TPU:15 before, /device:TPU:56 now
where the time goes in v2:
time: 65.4 us; the launch traced here: 65.2 us
  Pallas kernels  64.6 us (99%)
    pallas_call x1, Pallas kernels, on_device(): pl.pallas_call(functools.partial(kernel, sizes), out_shape=(jax.ShapeDtyp...  63 us
    pallas_call x1, Pallas kernels, on_device(): pl.pallas_call(write_out, out_shape=(jax.ShapeDtypeStruct(smooth.shape, f...  1.58 us

profile of v2, /device:TPU:56, one launch (start us, length us, event | category | flops | bytes accessed | tf_op | source)
XLA Modules:
  0.0 65.2 jit_solution(9262609098090215437)
XLA Ops:
  0.6 63.0 %shard_map.77 = (f32[256,128]{1,0:T(8,128)}, f32[4,768]{1,0:T(4,128)}) custom-call(f32[256,128]{1,0:T(8,128)} %bitcast.3, bf16[768,16,128]{2,1,0:T(8,128)(2,1)} %rows_hbm.1, s32[16,128]{1,0:T(8,128)} %ids_ref.1, f32[16]{0:T(128)} %mat_diag.1, f32[16]{0:T(128)} %mat_cond.1, f32[9]{0:T(128)} %coef.1), custom_call_target="tpu_custom_call" | custom-call | tf_op jit(solution)/shard_map/pallas_call | solution.py:438
  63.6 1.6 %shard_map.78 = (f32[256,128]{1,0:T(8,128)}, f32[4,768]{1,0:T(4,128)}) custom-call(f32[256,128]{1,0:T(8,128)} %get-tuple-element.6.smooth, f32[4,768]{1,0:T(4,128)} %get-tuple-element.7.panel), custom_call_target="tpu_custom_call" | custom-call | tf_op jit(solution)/shard_map/pallas_call | solution.py:478

commit v3 on v2

--- a/solution.py
+++ b/solution.py
@@ -144,9 +144,10 @@
                         acc[a - DEG : b - DEG, t] = acc[a - DEG : b - DEG, t] + coef[k] * value
 
 
-def finish(acc, unscaled, smooth, cols, nx):
+def finish(part, acc, unscaled, smooth, cols, nx):
     depth = cols.shape[-1]
-    for x in range(nx):
+    count = depth // LANES
+    for x in range(part * count, (part + 1) * count):
         done = []
         for g in range(2):
             value = acc[x, g] * unscaled[g, x]
@@ -206,6 +207,12 @@
     def greet(*device):
         pl.semaphore_signal(barrier, inc=1, device_id=device, device_id_type=MESH)
 
+    for dx in (-1, 1):
+        for dy in (-1, 1):
+            greet(lax.rem(me_x + nsx + dx, nsx), lax.rem(me_y + nsy + dy, nsy), me_z)
+    first_low, last_low = me_low == 0, me_low == low - 1
+    pl.when(first_low)(functools.partial(greet, lax.rem(me_x + nsx - 1, nsx), me_y, me_z))
+    pl.when(last_low)(functools.partial(greet, lax.rem(me_x + 1, nsx), me_y, me_z))
     greet(*up)
     greet(*down)
     for q in range(low):
@@ -213,12 +220,6 @@
     for h in range(2):
         for y in range(nsy):
             pl.when((h != me_high) | (y != me_y))(functools.partial(greet, h * low + me_low, y, me_z))
-    for dx in (-1, 1):
-        for dy in (-1, 1):
-            greet(lax.rem(me_x + nsx + dx, nsx), lax.rem(me_y + nsy + dy, nsy), me_z)
-    first_low, last_low = me_low == 0, me_low == low - 1
-    pl.when(first_low)(functools.partial(greet, lax.rem(me_x + nsx - 1, nsx), me_y, me_z))
-    pl.when(last_low)(functools.partial(greet, lax.rem(me_x + 1, nsx), me_y, me_z))
     peers = 2 + (low - 1) + (2 * nsy - 1) + 4
 
     own_cond(ids_ref, mat_cond, scaled, unscaled)
@@ -294,7 +295,6 @@
     unpack_edges(got, side)
     widen_edges(thin_got, main, nx)
     filter_steps(main, side, diag2, cond2, acc, coef, nx)
-    finish(acc, unscaled, smooth, cols, nx)
 
     def hop(way, s, p):
         last = s == steps
@@ -308,8 +308,10 @@
         return [(way, p) for p in range(PIECES) for way in range(2)
                 if s < steps or p % 2 == way]
 
-    for way, p in hops(1):
-        hop(way, 1, p).start()
+    for p in range(PIECES):
+        finish(p, acc, unscaled, smooth, cols, nx)
+        for way in range(2):
+            hop(way, 1, p).start()
     load_rows.wait()
     turn_rows(raw, flat)
 

time: 65.4 us -> 65.6 us (level)
  no operation moved by 1% of the time
where the time goes in v3:
time: 65.6 us; the launch traced here: 65.1 us
  Pallas kernels  64.5 us (98%)
    pallas_call x1, Pallas kernels, on_device(): pl.pallas_call(functools.partial(kernel, sizes), out_shape=(jax.ShapeDtyp...  62.9 us
    pallas_call x1, Pallas kernels, on_device(): pl.pallas_call(write_out, out_shape=(jax.ShapeDtypeStruct(smooth.shape, f...  1.58 us

profile of v3, /device:TPU:56, one launch (start us, length us, event | category | flops | bytes accessed | tf_op | source)
XLA Modules:
  0.0 65.1 jit_solution(12326527682676965902)
XLA Ops:
  0.6 62.9 %shard_map.77 = (f32[256,128]{1,0:T(8,128)}, f32[4,768]{1,0:T(4,128)}) custom-call(f32[256,128]{1,0:T(8,128)} %bitcast.3, bf16[768,16,128]{2,1,0:T(8,128)(2,1)} %rows_hbm.1, s32[16,128]{1,0:T(8,128)} %ids_ref.1, f32[16]{0:T(128)} %mat_diag.1, f32[16]{0:T(128)} %mat_cond.1, f32[9]{0:T(128)} %coef.1), custom_call_target="tpu_custom_call" | custom-call | tf_op jit(solution)/shard_map/pallas_call | solution.py:440
  63.5 1.6 %shard_map.78 = (f32[256,128]{1,0:T(8,128)}, f32[4,768]{1,0:T(4,128)}) custom-call(f32[256,128]{1,0:T(8,128)} %get-tuple-element.6.smooth, f32[4,768]{1,0:T(4,128)} %get-tuple-element.7.panel), custom_call_target="tpu_custom_call" | custom-call | tf_op jit(solution)/shard_map/pallas_call | solution.py:480

commit v4 on v2

--- a/solution.py
+++ b/solution.py
@@ -323,32 +323,32 @@
         s = (slot + 1) // 2
         return lax.rem(me_z + ncr - s, ncr) if slot % 2 else lax.rem(me_z + s, ncr)
 
-    def multiply(first, last):
+    def multiply(first, last, at=slice(None)):
         count = (last - first) * nc
         depth = cols.shape[-1]
         total = None
         for p in range(PIECES):
             lhs = cols[p, first:last].reshape(count, depth)
-            rhs = flat[:, p * depth : (p + 1) * depth]
+            rhs = flat[at, p * depth : (p + 1) * depth]
             part = lax.dot_general(lhs, rhs, (((1,), (1,)), ((), ())), preferred_element_type=jnp.float32)
             total = part if total is None else total + part
-        out_a[first:last] = total.astype(jnp.bfloat16).reshape(last - first, nc, flat.shape[0])
-
-    def send_a(slot):
+        out_a[first:last, :, at] = total.astype(jnp.bfloat16).reshape(last - first, nc, total.shape[1])
+
+    def send_a(slot, at=slice(None)):
         block = block_of(slot)
         to_low, high = lax.rem(block, low), block // low
         return to_low, high, pltpu.make_async_remote_copy(
-            src_ref=out_a.at[slot], dst_ref=in_a.at[high, me_low], send_sem=a_send.at[slot],
+            src_ref=out_a.at[slot, :, at], dst_ref=in_a.at[high, me_low, :, at], send_sem=a_send.at[slot],
             recv_sem=a_recv.at[high, me_low], device_id=(me_high * low + to_low, me_y, me_z), device_id_type=MESH)
 
-    def share(first, last):
+    def share(first, last, at=slice(None)):
         for slot in range(first, last):
-            to_low, high, copy = send_a(slot)
+            to_low, high, copy = send_a(slot, at)
             pl.when(to_low != me_low)(copy.start)
 
             @pl.when(to_low == me_low)
             def _(slot=slot, high=high):
-                in_a[high, me_low] = out_a[slot]
+                in_a[high, me_low, :, at] = out_a[slot, :, at]
 
     def send_b(h, y):
         return pltpu.make_async_remote_copy(
@@ -383,8 +383,14 @@
         first = 0 if s == 1 else 2 * s - 1
         last = min(2 * s + 1, 2 * steps)
         arrive(s)
-        multiply(first, last)
-        share(first, last)
+        if s < steps:
+            multiply(first, last)
+            share(first, last)
+        else:
+            for start in range(0, flat.shape[0], 256):
+                at = slice(start, min(start + 256, flat.shape[0]))
+                multiply(first, last, at)
+                share(first, last, at)
         if s == steps - 1:
             gather_a(early)
     gather_a(1 - early)

time: 65.4 us -> 65.8 us (level)
  no operation moved by 1% of the time
where the time goes in v4:
time: 65.8 us; the launch traced here: 65.6 us
  Pallas kernels  65 us (99%)
    pallas_call x1, Pallas kernels, on_device(): pl.pallas_call(functools.partial(kernel, sizes), out_shape=(jax.ShapeDtyp...  63.4 us
    pallas_call x1, Pallas kernels, on_device(): pl.pallas_call(write_out, out_shape=(jax.ShapeDtypeStruct(smooth.shape, f...  1.58 us

profile of v4, /device:TPU:56, one launch (start us, length us, event | category | flops | bytes accessed | tf_op | source)
XLA Modules:
  0.0 65.6 jit_solution(7966930943528479697)
XLA Ops:
  0.6 63.4 %shard_map.77 = (f32[256,128]{1,0:T(8,128)}, f32[4,768]{1,0:T(4,128)}) custom-call(f32[256,128]{1,0:T(8,128)} %bitcast.3, bf16[768,16,128]{2,1,0:T(8,128)(2,1)} %rows_hbm.1, s32[16,128]{1,0:T(8,128)} %ids_ref.1, f32[16]{0:T(128)} %mat_diag.1, f32[16]{0:T(128)} %mat_cond.1, f32[9]{0:T(128)} %coef.1), custom_call_target="tpu_custom_call" | custom-call | tf_op jit(solution)/shard_map/pallas_call | solution.py:444
  64.0 1.6 %shard_map.78 = (f32[256,128]{1,0:T(8,128)}, f32[4,768]{1,0:T(4,128)}) custom-call(f32[256,128]{1,0:T(8,128)} %get-tuple-element.6.smooth, f32[4,768]{1,0:T(4,128)} %get-tuple-element.7.panel), custom_call_target="tpu_custom_call" | custom-call | tf_op jit(solution)/shard_map/pallas_call | solution.py:484
